TPU v7x, 32 devices: a whole 2x2x4 slice. The times are simulated.
32 devices in a mesh: groups: 2 (over y), ranks: 4 (over z), tensor: 4 (over x, core).
Axes of the slice: x: 2, y: 2, z: 4, core: 2. Of those that a mesh axis runs over, the one named last changes fastest.
Arguments:
- queries: bfloat16 [32, 8192], P(('groups', 'ranks'), 'tensor'), parts along dimension 0, may hold values from -180 to 180
- cache: bfloat16 [32, 2, 1024, 1024], P(('groups', 'ranks'), None, None, 'tensor'), parts along dimension 0, may hold values from -7 to 7
- pages: bfloat16 [256, 2, 128, 1024], P(('groups', 'ranks'), None, None, 'tensor'), parts along dimension 0, may hold values from -6 to 6
- page_owner: int32 [256], P('groups'), parts along dimension 0, may hold values from 0 to 3, as said below
- page_slot: int32 [256], P('groups'), parts along dimension 0, may hold values from 0 to 31, as said below
- lengths: int32 [32], P(('groups', 'ranks')), parts along dimension 0, may hold values from 2 to 1024, as said below
- out_weight: bfloat16 [8192, 8192], P('tensor', 'ranks'), may hold values from -0.0625 to 0.0625
Outputs:
- layer_out: bfloat16 [32, 8192], P(('groups', 'tensor'), 'ranks'), parts along dimension 0
There are 2 independent parts, one for each index of `groups`. A program takes and returns all parts, laid end to end along the dimension named above; an argument that names none is the same for every part. Nothing has to cross between parts.
Inputs may be any that keep to these rules, and one draw needn't show every extreme that they name: `page_owner`: rows r * 32 to (r + 1) * 32 - 1 are the pages made on rank r; a rank sends either no page or exactly 8 pages to an owner, and every owner receives exactly 32 pages in all. `page_slot`: over the 32 pages that one owner receives, the slots are 0 to 31, each once. `lengths`: some sequence reaches 1024.
All inputs are finite; a program needn't handle non-finite values.
Results may differ from a plain program's by a relative error of at most 0.012.
Values may be sent and summed in bfloat16 or wider, within the bound.
A program may use at most 128 MiB of HBM per device.

v0:
```python
import jax
import jax.numpy as jnp
from jax import lax
from jax.sharding import PartitionSpec as P

HEAD = 128


def page_tables(page_owner, page_slot, rank_count, my_rank, capacity):
    page_count = page_owner.shape[0] // rank_count
    owners = page_owner.reshape(rank_count, page_count)
    slots = page_slot.reshape(rank_count, page_count)
    position = jnp.arange(page_count)
    earlier = position[None, :] < position[:, None]
    same_owner = owners[:, :, None] == owners[:, None, :]
    order_rank = jnp.sum(jnp.logical_and(same_owner, earlier[None]).astype(jnp.int32), axis=2)
    own_owner = lax.dynamic_index_in_dim(owners, my_rank, 0, keepdims=False)
    own_slot = lax.dynamic_index_in_dim(slots, my_rank, 0, keepdims=False)
    own_order = lax.dynamic_index_in_dim(order_rank, my_rank, 0, keepdims=False)
    page_bucket = own_owner * capacity + own_order
    buckets = jnp.arange(rank_count * capacity)
    send_match = page_bucket[None, :] == buckets[:, None]
    send_filled = jnp.any(send_match, axis=1)
    send_page = jnp.argmax(send_match, axis=1)
    owned = owners == my_rank
    columns = jnp.arange(capacity)
    recv_match = owned[:, None, :] & (order_rank[:, None, :] == columns[None, :, None])
    recv_filled = jnp.any(recv_match, axis=2).reshape(-1)
    chosen = jnp.argmax(recv_match, axis=2)
    bucket_slot = jnp.take_along_axis(slots, chosen, axis=1).reshape(-1)
    slot_match = (bucket_slot[None, :] == position[:, None]) & recv_filled[None, :]
    recv_row = jnp.argmax(slot_match, axis=1)
    return (
        own_owner,
        own_slot,
        page_bucket,
        send_filled,
        send_page,
        recv_filled,
        bucket_slot,
        recv_row,
    )


def to_buckets(values, filled, source, rank_count):
    picked = jnp.take(values, source, axis=0)
    shaped = filled.reshape((-1,) + (1,) * (values.ndim - 1))
    picked = jnp.where(shaped, picked, jnp.zeros_like(picked))
    return picked.reshape((rank_count, -1) + values.shape[1:])


def from_buckets(arrived, target):
    flattened = arrived.reshape((-1,) + arrived.shape[2:])
    return jnp.take(flattened, target, axis=0)


def per_device(queries, cache, pages, page_owner, page_slot, lengths, out_weight):
    rank_count = lax.axis_size("ranks")
    my_rank = lax.axis_index("ranks")
    seq_count = queries.shape[0]
    page_count = pages.shape[0]
    per_sequence = page_count // seq_count
    capacity = min(page_count, max(2, page_count // rank_count))
    page_size = pages.shape[2]
    kv_local = cache.shape[-1] // HEAD
    heads_local = queries.shape[1] // HEAD
    group_size = heads_local // kv_local
    resident = cache.shape[2]
    score_scale = HEAD ** (-0.5)
    tables = page_tables(page_owner, page_slot, rank_count, my_rank, capacity)
    own_owner, own_slot, page_bucket, send_filled, send_page, recv_filled, bucket_slot, recv_row = (
        tables
    )
    query_grid = queries.reshape(seq_count, kv_local, group_size, HEAD)
    res_keys = cache[:, 0].reshape(seq_count, resident, kv_local, HEAD)
    res_values = cache[:, 1].reshape(seq_count, resident, kv_local, HEAD)
    res_scores = (
        jnp.einsum("shgd,slhd->shgl", query_grid, res_keys, preferred_element_type=jnp.float32)
        * score_scale
    )
    position = jnp.arange(resident)
    live_mask = position[None, None, None, :] < lengths[:, None, None, None]
    res_scores = jnp.where(live_mask, res_scores, -jnp.inf)
    outgoing = to_buckets(pages, send_filled, send_page, rank_count)
    arrived = lax.all_to_all(outgoing, "ranks", split_axis=0, concat_axis=0, tiled=True)
    fresh_pages = from_buckets(arrived, recv_row).reshape(
        seq_count, per_sequence, 2, page_size, kv_local, HEAD
    )
    new_keys = fresh_pages[:, :, 0].reshape(seq_count, per_sequence * page_size, kv_local, HEAD)
    new_values = fresh_pages[:, :, 1].reshape(seq_count, per_sequence * page_size, kv_local, HEAD)
    new_scores = (
        jnp.einsum("shgd,slhd->shgl", query_grid, new_keys, preferred_element_type=jnp.float32)
        * score_scale
    )
    scores = jnp.concatenate([res_scores, new_scores], axis=3)
    row_peak = jnp.max(scores, axis=3, keepdims=True)
    exp_scores = jnp.exp(scores - row_peak)
    row_total = jnp.sum(exp_scores, axis=3, keepdims=True)
    weights = exp_scores.astype(jnp.bfloat16)
    res_weights = weights[..., :resident]
    new_weights = weights[..., resident:]
    res_sums = jnp.einsum(
        "shgl,slhd->shgd", res_weights, res_values, preferred_element_type=jnp.float32
    )
    new_sums = jnp.einsum(
        "shgl,slhd->shgd", new_weights, new_values, preferred_element_type=jnp.float32
    )
    attended = (
        ((res_sums + new_sums) / row_total)
        .astype(jnp.bfloat16)
        .reshape(seq_count, heads_local * HEAD)
    )
    terms = jnp.dot(
        lax.all_gather(attended, "ranks", axis=0, tiled=True),
        out_weight,
        preferred_element_type=jnp.float32,
    )
    return lax.psum_scatter(terms.astype(jnp.bfloat16), "tensor", scatter_dimension=0, tiled=True)


def solution(mesh):
    placed = (
        P(("groups", "ranks"), "tensor"),
        P(("groups", "ranks"), None, None, "tensor"),
        P(("groups", "ranks"), None, None, "tensor"),
        P("groups"),
        P("groups"),
        P(("groups", "ranks")),
        P("tensor", "ranks"),
    )
    return jax.shard_map(
        per_device,
        mesh=mesh,
        in_specs=placed,
        out_specs=P(("groups", "tensor"), "ranks"),
        check_vma=False,
    )
```

profile of v0, /device:TPU:0, one launch (start us, length us, event | category | flops | bytes accessed | tf_op | source)
XLA Modules:
  0.0 208.8 jit_solution(17673354705779305435)
XLA Ops:
  6.5 0.7 reshape.97
  7.3 0.2 convert_reduce_fusion
  7.5 0.6 iota_reduce_fusion.2
  8.2 0.1 fusion.12
  8.3 5.0 %gather_fusion.1 = bf16[32,2,128,256]{3,2,1,0:T(8,128)(2,1)} fusion(bf16[32,2,128,256]{3,2,1,0:T(8,128)(2,1)} %param.11, s32[1024]{0:T(1024)S(1)} %pad_clamp_fusion.1), kind=kCustom, calls=%fused_computation.clone | custom fusion | bytes 8388736 | tf_op jit(solution)/shard_map/jit(_take)/gather | solution.py:46
  13.3 4.7 %select_select_fusion = bf16[32,2,128,256]{3,2,1,0:T(8,128)(2,1)} fusion(bf16[32,2,128,256]{3,2,1,0:T(8,128)(2,1)} %gather_fusion.1, pred[32]{0:T(512)(128)(4,1)S(1)} %compare_and_fusion.1, pred[32]{0:T(512)(128)(4,1)S(1)} %fusion.12), kind=kLoop, calls=%fused_computation.3 | loop fusion | flops 4194304 | bytes 8388672 | tf_op jit(solution)/shard_map/jit(_where)/select_n | solution.py:48
  18.0 0.0 copy-start.1
  18.0 6.4 %all-to-all-start = ((bf16[4,8,2,128,256]{4,3,2,1,0:T(8,128)(2,1)}), bf16[4,8,2,128,256]{4,3,2,1,0:T(8,128)(2,1)}, u32[]{:S(2)}, u32[]{:S(2)}) async-start(bf16[4,8,2,128,256]{4,3,2,1,0:T(8,128)(2,1)} %bitcast.35), calls=%async_computation | async-start | bytes 8388608 | tf_op jit(solution)/shard_map/all_to_all | solution.py:85
  24.4 0.0 all-reduce.3.cloned.1.call-start
  24.4 0.7 iota_reduce_fusion.1
  25.2 0.1 reshape.120
  25.2 0.0 copy-done.1
  25.3 0.1 reshape.100
  25.3 0.8 gather_fusion
  26.1 0.1 reshape.123
  26.2 0.1 select_n.50
  26.3 0.1 fusion.14
  26.4 0.1 and.46
  26.5 3.9 %fusion.19 = (bf16[4,1,1024,256]{3,2,1,0:T(8,128)(2,1)S(1)}, bf16[4,1,1024,256]{3,2,1,0:T(8,128)(2,1)}) fusion(bf16[4,2,1024,256]{3,2,1,0:T(8,128)(2,1)} %param.10), kind=kLoop, calls=%fused_computation.50 | loop fusion | bytes 8388608 | tf_op jit(solution)/shard_map/slice | solution.py:75
  30.4 0.0 copy-start.2
  30.4 0.0 copy-start
  30.4 2.4 %copy.37 = bf16[4,1,1024,256]{2,3,0,1:T(8,128)(2,1)} copy(bf16[4,1,1024,256]{3,2,1,0:T(8,128)(2,1)S(1)} %get-tuple-element.14) | data formatting | bytes 4194304
  32.8 3.0 %copy.38 = bf16[4,1,1024,256]{2,3,0,1:T(8,128)(2,1)S(1)} copy(bf16[4,1,1024,256]{3,2,1,0:T(8,128)(2,1)} %get-tuple-element.15) | data formatting | bytes 4194304
  35.8 0.6 iota_reduce_fusion
  36.5 0.0 copy-done.2
  36.5 0.1 iota_compare_fusion.4
  36.6 0.0 copy-done
  36.6 2.1 fusion.20
  38.6 79.2 %all-to-all-done = bf16[4,8,2,128,256]{4,3,2,1,0:T(8,128)(2,1)} async-done(((bf16[4,8,2,128,256]{4,3,2,1,0:T(8,128)(2,1)}), bf16[4,8,2,128,256]{4,3,2,1,0:T(8,128)(2,1)}, u32[]{:S(2)}, u32[]{:S(2)}) %all-to-all-start) | async-done | bytes 4194336 | tf_op jit(solution)/shard_map/all_to_all | solution.py:85
  117.8 5.0 %gather_fusion.2 = bf16[32,2,128,256]{3,2,1,0:T(8,128)(2,1)} fusion(bf16[32,2,128,256]{3,2,1,0:T(8,128)(2,1)} %bitcast.4, s32[1024]{0:T(1024)S(1)} %pad_clamp_fusion), kind=kCustom, calls=%fused_computation.1.clone | custom fusion | bytes 8388736 | tf_op jit(solution)/shard_map/jit(_take)/gather | solution.py:54
  122.8 4.6 %broadcast_select_fusion = bf16[32,2,128,256]{3,2,1,0:T(8,128)(2,1)} fusion(bf16[32,2,128,256]{3,2,1,0:T(8,128)(2,1)} %gather_fusion.2, pred[32]{0:T(512)(128)(4,1)S(1)} %compare_and_fusion), kind=kLoop, calls=%fused_computation.4 | loop fusion | flops 2097152 | bytes 8388640 | tf_op jit(solution)/shard_map/jit(_take)/select_n | solution.py:54
  127.4 6.4 %copy.30 = bf16[32,2,128,256]{2,3,1,0:T(8,128)(2,1)} copy(bf16[32,2,128,256]{3,2,1,0:T(8,128)(2,1)} %broadcast_select_fusion) | data formatting | bytes 8388608 | tf_op jit(solution)/shard_map/jit(_take)/select_n | solution.py:54
  133.8 4.8 %fusion.18 = (bf16[4,8,1,128,2,128]{3,5,4,2,1,0:T(8,128)(2,1)}, bf16[4,8,1,128,2,128]{3,5,4,2,1,0:T(8,128)(2,1)}) fusion(bf16[4,8,2,128,2,128]{3,5,4,2,1,0:T(8,128)(2,1)} %bitcast.36), kind=kLoop, calls=%fused_computation.49 | loop fusion | bytes 8388608 | tf_op jit(solution)/shard_map/slice | solution.py:90
  138.6 4.0 %copy.31 = bf16[4,8,1,128,2,128]{5,3,1,4,0,2:T(8,128)(2,1)} copy(bf16[4,8,1,128,2,128]{3,5,4,2,1,0:T(8,128)(2,1)} %get-tuple-element.13) | data formatting | bytes 4194304 | tf_op jit(solution)/shard_map/slice | solution.py:89
  142.6 2.3 %fusion.21 = (f32[4,2,8]{2,1,0:T(2,128)S(1)}, f32[4,2,8,1024]{3,2,1,0:T(8,128)S(1)}) fusion(bf16[4,1024,2,128]{3,1,2,0:T(8,128)(2,1)} %bitcast.40, bf16[1,4,16,128]{3,1,2,0:T(4,128)(2,1)S(1)} %bitcast.42), kind=kOutput, calls=%fused_computation.52 | convolution fusion | flops 16908224 | bytes 2375936 | tf_op jit(solution)/shard_map/shgd,slhd->shgl/dot_general | solution.py:92
  144.9 4.0 %copy.34 = bf16[4,8,1,128,2,128]{5,3,1,4,0,2:T(8,128)(2,1)} copy(bf16[4,8,1,128,2,128]{3,5,4,2,1,0:T(8,128)(2,1)} %get-tuple-element.12) | data formatting | bytes 4194304 | tf_op jit(solution)/shard_map/slice | solution.py:90
  148.9 0.2 fusion.5
  149.1 0.6 fusion.8
  149.8 2.0 fusion.3
  151.8 13.2 %all-gather = bf16[4,4,2048]{2,1,0:T(4,128)(2,1)S(1)} all-gather(bf16[1,4,2048]{2,1,0:T(4,128)(2,1)S(1)} %reshape.133), channel_id=1, replica_groups=mesh['groups'=2,'ranks'=4,'tensor'=4] {'ranks'}, dimensions={0}, use_global_device_ids=true | all-gather | bytes 81920 | tf_op jit(solution)/shard_map/all_gather | solution.py:114
  165.0 0.0 copy-start.3
  165.0 5.2 %convolution_convert_fusion = bf16[16,2048]{1,0:T(8,128)(2,1)} fusion(bf16[16,2048]{1,0:T(8,128)(2,1)S(1)} %reshape.134, bf16[2048,2048]{1,0:T(8,128)(2,1)} %param.15), kind=kOutput, calls=%fused_computation.5 | convolution fusion | flops 134250496 | bytes 8519680 | tf_op jit(solution)/shard_map/dot_general | solution.py:113
  170.2 0.0 all-reduce.3.cloned.1.call-update
  170.3 0.0 copy-done.3
  170.3 0.6 dynamic-slice
  171.5 29.0 %all-reduce.3.cloned.1.call-done = bf16[16,2048]{1,0:T(8,128)(2,1)} async-done(((bf16[16,2048]{1,0:T(8,128)(2,1)}), bf16[16,2048]{1,0:T(8,128)(2,1)}) %all-reduce.3.cloned.1.call-update) | async-done | bytes 65552
  200.5 1.4 constant_dynamic-slice_fusion
  (14 shorter events, 0.1 us)
Async XLA Ops:
  18.0 7.3 %copy-start.1 = (s32[128]{0:T(128)S(1)}, s32[128]{0:T(128)}, u32[]{:S(2)}) copy-start(s32[128]{0:T(128)} %param.13) | copy-start | bytes 1540
  18.0 99.9 %all-to-all-start = ((bf16[4,8,2,128,256]{4,3,2,1,0:T(8,128)(2,1)}), bf16[4,8,2,128,256]{4,3,2,1,0:T(8,128)(2,1)}, u32[]{:S(2)}, u32[]{:S(2)}) async-start(bf16[4,8,2,128,256]{4,3,2,1,0:T(8,128)(2,1)} %bitcast.35), calls=%async_computation | async-start | bytes 8388608 | tf_op jit(solution)/shard_map/all_to_all | solution.py:85
  24.4 176.1 %all-reduce.3.cloned.1.call-start = ((), (), s32[]{:S(2)}) async-start(), calls=%async_computation.1 | async-start | bytes 131072
  30.4 6.1 %copy-start.2 = (s32[4]{0:T(128)S(1)}, s32[4]{0:T(128)}, u32[]{:S(2)}) copy-start(s32[4]{0:T(128)} %param.14) | copy-start | bytes 52
  30.4 6.1 %copy-start = (bf16[4,2048]{1,0:T(4,128)(2,1)S(1)}, bf16[4,2048]{1,0:T(4,128)(2,1)}, u32[]{:S(2)}) copy-start(bf16[4,2048]{1,0:T(4,128)(2,1)} %param.9) | copy-start | bytes 49156
  165.0 5.2 %copy-start.3 = (u32[32]{0:T(128)S(1)}, u32[32]{0:T(128)}, u32[]{:S(2)}) copy-start(u32[32]{0:T(128)} %constant.79) | copy-start | bytes 388
Sparse Core Ops, SparseCore 0:
  170.4 30.1 all-reduce.2
where the time goes:
time: 210 us; the launch traced here: 209 us
  waiting for transfers between devices  108 us (51%)
  local copies, waits for them, and re-layouts  42.3 us (20%)
  between operations  14.1 us (7%)
  blocking collectives  13.2 us (6%)
  other arithmetic  12.2 us (6%)
  matrix products  12.2 us (6%)
  starting transfers between devices  6.45 us (3%)
    all_to_all x1, waiting for transfers between devices, per_device(): lax.all_to_all(outgoing, 'ranks', split_axis=0, concat_axis=0, tiled=True)  79.2 us
    unnamed x2, waiting for transfers between devices  29.1 us
    all_gather x1, blocking collectives, per_device(): lax.all_gather(attended, 'ranks', axis=0, tiled=True)  13.2 us
    slice x2, local copies, waits for them, and re-layouts, per_device(): fresh_pages[:, :, 1]  8.76 us
    unnamed x14, local copies, waits for them, and re-layouts  7.41 us
    all_to_all x1, starting transfers between devices, per_device(): lax.all_to_all(outgoing, 'ranks', split_axis=0, concat_axis=0, tiled=True)  6.45 us
    select_n x1, local copies, waits for them, and re-layouts, from_buckets(): return jnp.take(flattened, target, axis=0)  6.42 us
    dot_general x1, matrix products, per_device(): jnp.dot(lax.all_gather(attended, 'ranks', axis=0, tiled=True), out_weight...  5.2 us
  transfers between devices with their start and end apart: 2, of which 2 were waited for; matrix products, arithmetic and copies ran while one was open for 7% of the time, Pallas kernels for 0%

commit v1 on v0

v1 whole, which is shorter than its diff:
```python
import functools

import jax
import jax.numpy as jnp
from jax import lax
from jax.experimental import pallas as pl
from jax.experimental.pallas import tpu as pltpu
from jax.sharding import PartitionSpec as P

HEAD = 128
MESH = pl.DeviceIdType.MESH
LOWEST = -1e30
W_PARTS = 4
PAGE_PARTS = 4


def kernel(
    ranks,
    tensors,
    seq_ref,
    table_ref,
    length_ref,
    q_ref,
    cache_hbm,
    pages_hbm,
    weight_hbm,
    out_ref,
    cache_v,
    pages_v,
    weight_v,
    q_recv,
    q_wide,
    part_o,
    part_m,
    part_l,
    o_send,
    o_recv,
    ml_send,
    ml_recv,
    att_send,
    att_recv,
    att_f32,
    att_wide,
    terms,
    sum_send,
    sum_recv,
    load_sem,
    q_sems,
    o_sems,
    ml_sems,
    att_sems,
    sum_sems,
):
    me = lax.axis_index("ranks")
    my_tensor = lax.axis_index("tensor")
    seqs, heads, _ = q_ref.shape
    pages = pages_v.shape[0]
    per_seq = pages // seqs
    resident = cache_v.shape[2]
    half = heads // 2
    all_seqs = ranks * seqs
    scale = HEAD ** (-0.5)
    rows = seqs * heads

    loads = []
    for j in range(seqs):
        loads.append(pltpu.make_async_copy(cache_hbm.at[j], cache_v.at[j], load_sem.at[j]))
    step = pages // PAGE_PARTS
    for j in range(PAGE_PARTS):
        span = pl.ds(j * step, step)
        loads.append(
            pltpu.make_async_copy(pages_hbm.at[span], pages_v.at[span], load_sem.at[seqs + j])
        )
    depth = weight_v.shape[0] // W_PARTS
    for j in range(W_PARTS):
        span = pl.ds(j * depth, depth)
        loads.append(
            pltpu.make_async_copy(
                weight_hbm.at[span], weight_v.at[span], load_sem.at[seqs + PAGE_PARTS + j]
            )
        )
    for load in loads:
        load.start()

    barrier = pltpu.get_barrier_semaphore()
    for d in range(1, ranks):
        pl.semaphore_signal(
            barrier, inc=1, device_id={"ranks": lax.rem(me + d, ranks)}, device_id_type=MESH
        )
    for d in range(1, tensors):
        pl.semaphore_signal(
            barrier,
            inc=1,
            device_id={"tensor": lax.rem(my_tensor + d, tensors)},
            device_id_type=MESH,
        )
    pl.semaphore_wait(barrier, ranks + tensors - 2)

    def to_rank(d, source, target, sems):
        return pltpu.make_async_remote_copy(
            src_ref=source,
            dst_ref=target.at[d],
            send_sem=sems.at[0, d],
            recv_sem=sems.at[1, d],
            device_id={"ranks": lax.rem(me + d, ranks)},
            device_id_type=MESH,
        )

    q_copies = [to_rank(d, q_ref, q_recv, q_sems) for d in range(1, ranks)]
    for copy in q_copies:
        copy.start()

    upper = lax.broadcasted_iota(jnp.int32, (heads, HEAD), 0) < half

    def widen(q):
        wide = q.astype(jnp.float32)
        zero = jnp.zeros_like(wide)
        return jnp.concatenate(
            [jnp.where(upper, wide, zero), jnp.where(upper, zero, wide)], axis=1
        ).astype(jnp.bfloat16)

    def score(q, keys):
        return (
            lax.dot_general(q, keys, (((1,), (1,)), ((), ())), preferred_element_type=jnp.float32)
            * scale
        )

    def finish(scores, values, slot):
        peak = jnp.max(scores, axis=1, keepdims=True)
        exps = jnp.exp(scores - peak)
        total = jnp.sum(exps, axis=1, keepdims=True)
        mix = jnp.dot(exps.astype(jnp.bfloat16), values, preferred_element_type=jnp.float32)
        part_o[slot] = jnp.where(upper, mix[:, :HEAD], mix[:, HEAD:])
        part_m[slot] = jnp.broadcast_to(peak, (heads, HEAD))
        part_l[slot] = jnp.broadcast_to(total, (heads, HEAD))

    for j in range(seqs):
        q_wide[me * seqs + j] = widen(q_ref[j])
    part_o[pages] = jnp.zeros((heads, HEAD), jnp.float32)
    part_m[pages] = jnp.full((heads, HEAD), LOWEST, jnp.float32)
    part_l[pages] = jnp.zeros((heads, HEAD), jnp.float32)
    position = lax.broadcasted_iota(jnp.int32, (heads, resident), 1)
    for j in range(seqs):
        loads[j].wait()
        scores = score(q_wide[me * seqs + j], cache_v[j, 0])
        scores = jnp.where(position < length_ref[j], scores, -jnp.inf)
        finish(scores, cache_v[j, 1], pages + 1 + j)

    for d in range(1, ranks):
        q_copies[d - 1].wait_recv()
        source = lax.rem(me - d + ranks, ranks)
        for j in range(seqs):
            q_wide[source * seqs + j] = widen(q_recv[d, j])

    for j in range(PAGE_PARTS):
        loads[seqs + j].wait()

        for i in range(step):
            page = j * step + i
            finish(score(q_wide[seq_ref[page]], pages_v[page, 0]), pages_v[page, 1], page)

    lane = lax.broadcasted_iota(jnp.int32, (rows, HEAD), 1)
    row = lax.broadcasted_iota(jnp.int32, (rows, HEAD), 0)
    low_diagonal = lane == row
    high_diagonal = lane == row + rows

    def gather_owner(owner):
        peaks, totals, sums = [], [], []
        for j in range(seqs):
            slots = [table_ref[(owner * seqs + j) * per_seq + k] for k in range(per_seq)]
            slot_peaks = [part_m[slot] for slot in slots]
            peak = functools.reduce(jnp.maximum, slot_peaks)
            factors = [jnp.exp(one - peak) for one in slot_peaks]
            peaks.append(peak)
            totals.append(sum(f * part_l[slot] for f, slot in zip(factors, slots)))
            sums.append(sum(f * part_o[slot] for f, slot in zip(factors, slots)))
        return [jnp.concatenate(x, axis=0) for x in (peaks, totals, sums)]

    o_copies, ml_copies = [], []
    for d in range(1, ranks):
        peak, total, mix = gather_owner(lax.rem(me + d, ranks))
        o_send[d] = mix.astype(jnp.bfloat16)
        packed = jnp.where(low_diagonal, peak, jnp.where(high_diagonal, total, 0.0))
        ml_send[d] = jnp.broadcast_to(jnp.sum(packed, axis=0, keepdims=True), (8, HEAD))
        o_copies.append(to_rank(d, o_send.at[d], o_recv, o_sems))
        ml_copies.append(to_rank(d, ml_send.at[d], ml_recv, ml_sems))
        ml_copies[-1].start()
        o_copies[-1].start()

    peak, total, mix = gather_owner(me)
    own = pl.ds(pages + 1, seqs)
    states = [
        (peak, total, mix),
        tuple(x[own].reshape(rows, HEAD) for x in (part_m, part_l, part_o)),
    ]

    def merge(a, b):
        top = jnp.maximum(a[0], b[0])
        fa, fb = jnp.exp(a[0] - top), jnp.exp(b[0] - top)
        return top, fa * a[1] + fb * b[1], fa * a[2] + fb * b[2]

    state = merge(*states)
    for d in range(1, ranks):
        ml_copies[d - 1].wait_recv()
        o_copies[d - 1].wait_recv()
        spread = jnp.broadcast_to(ml_recv[d, 0:1, :], (rows, HEAD))
        peak = jnp.sum(jnp.where(low_diagonal, spread, 0.0), axis=1, keepdims=True)
        total = jnp.sum(jnp.where(high_diagonal, spread, 0.0), axis=1, keepdims=True)
        state = merge(
            state,
            (
                jnp.broadcast_to(peak, (rows, HEAD)),
                jnp.broadcast_to(total, (rows, HEAD)),
                o_recv[d].astype(jnp.float32),
            ),
        )
    attended = (state[2] / state[1]).astype(jnp.bfloat16)
    att_send[...] = attended
    att_copies = [to_rank(d, att_send, att_recv, att_sems) for d in range(1, ranks)]
    for copy in att_copies:
        copy.start()

    def place(source, value):
        att_f32[pl.ds(source * seqs, seqs)] = value.astype(jnp.float32).reshape(seqs, heads, HEAD)

    place(me, attended)
    for d in range(1, ranks):
        att_copies[d - 1].wait_recv()
        place(lax.rem(me - d + ranks, ranks), att_recv[d])
    for h in range(heads):
        att_wide[:, h * HEAD : (h + 1) * HEAD] = att_f32[:, h, :].astype(jnp.bfloat16)

    for j in range(W_PARTS):
        loads[seqs + PAGE_PARTS + j].wait()
    width = weight_v.shape[1]
    block = min(width, 256)
    share = all_seqs // tensors

    @pl.loop(0, width // block)
    def _(n):
        span = pl.ds(pl.multiple_of(n * block, block), block)
        product = jnp.dot(att_wide[...], weight_v[:, span], preferred_element_type=jnp.float32)
        for t in range(tensors):
            terms[t, :, span] = product[t * share : (t + 1) * share]

    _, sum_rows, sum_cols = sum_send.shape
    folds = sum_rows // share

    def fold(t):
        chunk = terms[t]
        return jnp.concatenate(
            [chunk[:, c * sum_cols : (c + 1) * sum_cols] for c in range(folds)], axis=0
        )

    sum_copies = []
    for d in range(1, tensors):
        target = lax.rem(my_tensor + d, tensors)
        sum_send[d] = fold(target).astype(jnp.bfloat16)
        copy = pltpu.make_async_remote_copy(
            src_ref=sum_send.at[d],
            dst_ref=sum_recv.at[d],
            send_sem=sum_sems.at[0, d],
            recv_sem=sum_sems.at[1, d],
            device_id={"tensor": target},
            device_id_type=MESH,
        )
        copy.start()
        sum_copies.append(copy)
    result = fold(my_tensor)
    for d in range(1, tensors):
        sum_copies[d - 1].wait_recv()
        result = result + sum_recv[d].astype(jnp.float32)
    for c in range(folds):
        out_ref[:, c * sum_cols : (c + 1) * sum_cols] = result[
            c * share : (c + 1) * share
        ].astype(jnp.bfloat16)

    for copy in q_copies + o_copies + ml_copies + att_copies + sum_copies:
        copy.wait_send()


def per_device(queries, cache, pages, page_owner, page_slot, lengths, out_weight):
    ranks = lax.axis_size("ranks")
    tensors = lax.axis_size("tensor")
    me = lax.axis_index("ranks")
    seqs, width = queries.shape
    heads = width // HEAD
    page_count = pages.shape[0]
    kv_width = cache.shape[-1]
    resident = cache.shape[2]
    features = out_weight.shape[1]
    own = me * page_count
    place = lax.dynamic_slice_in_dim(
        page_owner * page_count + page_slot, own, page_count, 0
    )
    seq_of_page = place // (page_count // seqs)
    match = jnp.arange(ranks * page_count)[:, None] == place[None, :]
    table = jnp.min(jnp.where(match, jnp.arange(page_count)[None, :], page_count), axis=1)
    all_seqs = ranks * seqs
    share = all_seqs // tensors
    folds = max(1, 16 // share)
    rows = seqs * heads
    slots = page_count + 1 + seqs
    bf16, f32 = jnp.bfloat16, jnp.float32
    smem = pl.BlockSpec(memory_space=pltpu.SMEM)
    vmem = pl.BlockSpec(memory_space=pltpu.VMEM)
    hbm = pl.BlockSpec(memory_space=pl.ANY)
    sems = pltpu.SemaphoreType.DMA
    return pl.pallas_call(
        functools.partial(kernel, ranks, tensors),
        out_shape=jax.ShapeDtypeStruct((share, features), bf16),
        in_specs=[smem, smem, smem, vmem, hbm, hbm, hbm],
        out_specs=vmem,
        scratch_shapes=[
            pltpu.VMEM(cache.shape, bf16),
            pltpu.VMEM(pages.shape, bf16),
            pltpu.VMEM(out_weight.shape, bf16),
            pltpu.VMEM((ranks, seqs, heads, HEAD), bf16),
            pltpu.VMEM((all_seqs, heads, kv_width), bf16),
            pltpu.VMEM((slots, heads, HEAD), f32),
            pltpu.VMEM((slots, heads, HEAD), f32),
            pltpu.VMEM((slots, heads, HEAD), f32),
            pltpu.VMEM((ranks, rows, HEAD), bf16),
            pltpu.VMEM((ranks, rows, HEAD), bf16),
            pltpu.VMEM((ranks, 8, HEAD), f32),
            pltpu.VMEM((ranks, 8, HEAD), f32),
            pltpu.VMEM((rows, HEAD), bf16),
            pltpu.VMEM((ranks, rows, HEAD), bf16),
            pltpu.VMEM((all_seqs, heads, HEAD), f32),
            pltpu.VMEM((all_seqs, width), bf16),
            pltpu.VMEM((tensors, share, features), f32),
            pltpu.VMEM((tensors, share * folds, features // folds), bf16),
            pltpu.VMEM((tensors, share * folds, features // folds), bf16),
            sems((seqs + PAGE_PARTS + W_PARTS,)),
            sems((2, ranks)),
            sems((2, ranks)),
            sems((2, ranks)),
            sems((2, ranks)),
            sems((2, tensors)),
        ],
        compiler_params=pltpu.CompilerParams(
            collective_id=0, has_side_effects=True, vmem_limit_bytes=48 * 1024 * 1024
        ),
        cost_estimate=pl.CostEstimate(
            flops=2 * all_seqs * width * features,
            bytes_accessed=2 * (cache.size + pages.size + out_weight.size),
            transcendentals=0,
        ),
    )(
        seq_of_page,
        table,
        lengths,
        queries.reshape(seqs, heads, HEAD),
        cache,
        pages,
        out_weight,
    )


def solution(mesh):
    placed = (
        P(("groups", "ranks"), "tensor"),
        P(("groups", "ranks"), None, None, "tensor"),
        P(("groups", "ranks"), None, None, "tensor"),
        P("groups"),
        P("groups"),
        P(("groups", "ranks")),
        P("tensor", "ranks"),
    )
    return jax.shard_map(
        per_device,
        mesh=mesh,
        in_specs=placed,
        out_specs=P(("groups", "tensor"), "ranks"),
        check_vma=False,
    )
```

time: 210 us -> 35.7 us (0.17)
  waiting for transfers between devices: 108 us -> 0 us
  local copies, waits for them, and re-layouts: 42.3 us -> 4.17 us
  Pallas kernels: 0 us -> 30.4 us
  between operations: 14.1 us -> 0.01 us
  blocking collectives: 13.2 us -> 0 us
  matrix products: 12.2 us -> 0 us
  other arithmetic: 12.2 us -> 0.85 us
  starting transfers between devices: 6.45 us -> 0 us
    all_to_all x1 -> x0, waiting for transfers between devices: 79.2 us -> none  [per_device(): lax.all_to_all(outgoing, 'ranks', split_axis=0, concat_axis=0, tiled=True)]
    pallas_call x0 -> x1, Pallas kernels: none -> 30.4 us  [per_device(): pl.pallas_call(functools.partial(kernel, ranks, tensors), out_shape=jax.S...]
    unnamed x2 -> x0, waiting for transfers between devices: 29.1 us -> none
    slice x4 -> x0, local copies, waits for them, and re-layouts: 16.6 us -> none  [the longest x2 8.76 us: per_device(): fresh_pages[:, :, 1]]
    all_gather x1 -> x0, blocking collectives: 13.2 us -> none  [per_device(): lax.all_gather(attended, 'ranks', axis=0, tiled=True)]
    dot_general x5 -> x0, matrix products: 12.2 us -> none  [the longest x1 5.2 us: per_device(): jnp.dot(lax.all_gather(attended, 'ranks', axis=0, tiled=True), out_weight...]
    gather x5 -> x0, local copies, waits for them, and re-layouts: 10.9 us -> none  [the longest x1 4.97 us: to_buckets(): picked = jnp.take(values, source, axis=0)]
    select_n x5 -> x1, other arithmetic: 9.32 us -> 0.08 us  [per_device(): seq_of_page = place // (page_count // seqs)]
  transfers between devices with their start and end apart: 2 -> 0, of which waited for: 2 -> 0; matrix products, arithmetic and copies ran while one was open for 7% -> 0% of each run, Pallas kernels for 0% -> 0%
where the time goes in v1:
time: 35.7 us; the launch traced here: 35.5 us
  Pallas kernels  30.4 us (85%)
  local copies, waits for them, and re-layouts  4.17 us (12%)
  other arithmetic  0.85 us (2%)
    pallas_call x1, Pallas kernels, per_device(): pl.pallas_call(functools.partial(kernel, ranks, tensors), out_shape=jax.S...  30.4 us
    unnamed x6, local copies, waits for them, and re-layouts  4.17 us

profile of v1, /device:TPU:0, one launch (start us, length us, event | category | flops | bytes accessed | tf_op | source)
XLA Modules:
  0.0 35.5 jit_solution(11093254712011880705)
XLA Ops:
  0.0 0.7 %multiply_add_fusion = s32[128]{0:T(128)S(1)} fusion(s32[128]{0:T(128)} %param.11, s32[128]{0:T(128)} %param.10), kind=kLoop, calls=%fused_computation.7 | loop fusion | flops 256 | bytes 1536 | tf_op jit(solution)/shard_map/add | solution.py:294
  0.7 0.1 and_select_fusion
  0.8 0.1 select_reduce_fusion.table_ref
  0.8 0.7 %copy.10 = bf16[1,4,16,128]{3,2,1,0:T(8,128)(2,1)S(1)} copy(bf16[1,4,16,128]{3,1,2,0:T(4,128)(2,1)} %bitcast.5) | data formatting | bytes 32768
  1.6 0.0 copy-start
  1.6 2.2 %copy-done = bf16[4,2,1024,256]{3,2,1,0:T(8,128)(2,1)S(1)} copy-done((bf16[4,2,1024,256]{3,2,1,0:T(8,128)(2,1)S(1)}, bf16[4,2,1024,256]{3,2,1,0:T(8,128)(2,1)}, u32[]{:S(2)}) %copy-start) | copy-done | bytes 4194328
  3.8 0.0 copy-start.1
  3.8 0.7 %copy-done.1 = s32[4]{0:T(128)S(1)} copy-done((s32[4]{0:T(128)S(1)}, s32[4]{0:T(128)}, u32[]{:S(2)}) %copy-start.1) | copy-done | bytes 40
  4.4 30.4 %shard_map.73 = bf16[4,2048]{1,0:T(4,128)(2,1)S(1)} custom-call(s32[32]{0:T(128)S(1)} %get-tuple-element.5.seq_ref, s32[128]{0:T(128)S(1)} %select_reduce_fusion.table_ref, s32[4]{0:T(128)S(1)} %copy-done.1, bf16[4,16,128]{2,1,0:T(8,128)(2,1)S(1)} %bitcast.4, bf16[4,2,1024,256]{3,2,1,0:T(8,128)(2,1)S(1)} %copy-done, bf16[32,2,128,256]{3,2,1,0:T(8,128)(2,1)} %pages_hbm.1, ...), custom_call_target="tpu_custom_call" | custom-call | flops 134217728 | bytes 16777216 | tf_op jit(solution)/shard_map/pallas_call | solution.py:309
  34.9 0.6 %copy.12 = bf16[4,2048]{1,0:T(4,128)(2,1)} copy(bf16[4,2048]{1,0:T(4,128)(2,1)S(1)} %shard_map.73) | data formatting | bytes 32768
Async XLA Ops:
  1.6 2.2 %copy-start = (bf16[4,2,1024,256]{3,2,1,0:T(8,128)(2,1)S(1)}, bf16[4,2,1024,256]{3,2,1,0:T(8,128)(2,1)}, u32[]{:S(2)}) copy-start(bf16[4,2,1024,256]{3,2,1,0:T(8,128)(2,1)} %cache_hbm.1) | copy-start | bytes 12582916
  3.8 0.7 %copy-start.1 = (s32[4]{0:T(128)S(1)}, s32[4]{0:T(128)}, u32[]{:S(2)}) copy-start(s32[4]{0:T(128)} %length_ref.1) | copy-start | bytes 52

commit v2 on v1

--- a/solution.py
+++ b/solution.py
@@ -17,14 +17,21 @@
 def kernel(
     ranks,
     tensors,
-    seq_ref,
-    table_ref,
-    length_ref,
-    q_ref,
+    owner_hbm,
+    slot_hbm,
+    length_hbm,
+    query_ref,
     cache_hbm,
     pages_hbm,
     weight_hbm,
     out_ref,
+    owner_ref,
+    slot_ref,
+    length_ref,
+    table_v,
+    table_ref,
+    q_f32,
+    q_ref,
     cache_v,
     pages_v,
     weight_v,
@@ -44,6 +51,7 @@
     terms,
     sum_send,
     sum_recv,
+    meta_sem,
     load_sem,
     q_sems,
     o_sems,
@@ -62,6 +70,15 @@
     scale = HEAD ** (-0.5)
     rows = seqs * heads
 
+    metas = [
+        pltpu.make_async_copy(source, target, meta_sem.at[k])
+        for k, (source, target) in enumerate(
+            ((owner_hbm, owner_ref), (slot_hbm, slot_ref), (length_hbm, length_ref))
+        )
+    ]
+    for copy in metas:
+        copy.start()
+
     loads = []
     for j in range(seqs):
         loads.append(pltpu.make_async_copy(cache_hbm.at[j], cache_v.at[j], load_sem.at[j]))
@@ -79,7 +96,7 @@
                 weight_hbm.at[span], weight_v.at[span], load_sem.at[seqs + PAGE_PARTS + j]
             )
         )
-    for load in loads:
+    for load in loads[: seqs + PAGE_PARTS]:
         load.start()
 
     barrier = pltpu.get_barrier_semaphore()
@@ -94,6 +111,9 @@
             device_id={"tensor": lax.rem(my_tensor + d, tensors)},
             device_id_type=MESH,
         )
+    for h in range(heads):
+        q_f32[:, h, :] = query_ref[:, h * HEAD : (h + 1) * HEAD].astype(jnp.float32)
+    q_ref[...] = q_f32[...].astype(jnp.bfloat16)
     pl.semaphore_wait(barrier, ranks + tensors - 2)
 
     def to_rank(d, source, target, sems):
@@ -125,14 +145,33 @@
             * scale
         )
 
-    def finish(scores, values, slot):
-        peak = jnp.max(scores, axis=1, keepdims=True)
-        exps = jnp.exp(scores - peak)
+    def parts(count, scores, values, first):
+        block = jnp.concatenate(scores, axis=0)
+        peak = jnp.max(block, axis=1, keepdims=True)
+        exps = jnp.exp(block - peak)
         total = jnp.sum(exps, axis=1, keepdims=True)
-        mix = jnp.dot(exps.astype(jnp.bfloat16), values, preferred_element_type=jnp.float32)
-        part_o[slot] = jnp.where(upper, mix[:, :HEAD], mix[:, HEAD:])
-        part_m[slot] = jnp.broadcast_to(peak, (heads, HEAD))
-        part_l[slot] = jnp.broadcast_to(total, (heads, HEAD))
+        span = pl.ds(first, count)
+        shape = (count, heads, HEAD)
+        part_m[span] = jnp.broadcast_to(peak, (count * heads, HEAD)).reshape(shape)
+        part_l[span] = jnp.broadcast_to(total, (count * heads, HEAD)).reshape(shape)
+        exps = exps.astype(jnp.bfloat16)
+        for k in range(count):
+            mix = jnp.dot(
+                exps[k * heads : (k + 1) * heads], values(k), preferred_element_type=jnp.float32
+            )
+            part_o[first + k] = jnp.where(upper, mix[:, :HEAD], mix[:, HEAD:])
+
+    for copy in metas:
+        copy.wait()
+    spots = lax.broadcasted_iota(jnp.int32, table_v.shape, 0) * HEAD
+    spots = spots + lax.broadcasted_iota(jnp.int32, table_v.shape, 1)
+    table = jnp.full(table_v.shape, pages, jnp.int32)
+    for page in range(pages):
+        place = owner_ref[me * pages + page] * pages + slot_ref[me * pages + page]
+        table = jnp.where(spots == place, page, table)
+    table_v[...] = table
+    table_copy = pltpu.make_async_copy(table_v, table_ref, meta_sem.at[3])
+    table_copy.start()
 
     for j in range(seqs):
         q_wide[me * seqs + j] = widen(q_ref[j])
@@ -140,11 +179,19 @@
     part_m[pages] = jnp.full((heads, HEAD), LOWEST, jnp.float32)
     part_l[pages] = jnp.zeros((heads, HEAD), jnp.float32)
     position = lax.broadcasted_iota(jnp.int32, (heads, resident), 1)
+    scores = []
     for j in range(seqs):
         loads[j].wait()
-        scores = score(q_wide[me * seqs + j], cache_v[j, 0])
-        scores = jnp.where(position < length_ref[j], scores, -jnp.inf)
-        finish(scores, cache_v[j, 1], pages + 1 + j)
+        scores.append(
+            jnp.where(
+                position < length_ref[j],
+                score(q_wide[me * seqs + j], cache_v[j, 0]),
+                -jnp.inf,
+            )
+        )
+    for load in loads[seqs + PAGE_PARTS :]:
+        load.start()
+    parts(seqs, scores, lambda j: cache_v[j, 1], pages + 1)
 
     for d in range(1, ranks):
         q_copies[d - 1].wait_recv()
@@ -154,10 +201,12 @@
 
     for j in range(PAGE_PARTS):
         loads[seqs + j].wait()
-
-        for i in range(step):
-            page = j * step + i
-            finish(score(q_wide[seq_ref[page]], pages_v[page, 0]), pages_v[page, 1], page)
+        scores = []
+        for page in range(j * step, (j + 1) * step):
+            place = owner_ref[me * pages + page] * pages + slot_ref[me * pages + page]
+            scores.append(score(q_wide[place // per_seq], pages_v[page, 0]))
+        parts(step, scores, lambda k: pages_v[j * step + k, 1], j * step)
+    table_copy.wait()
 
     lane = lax.broadcasted_iota(jnp.int32, (rows, HEAD), 1)
     row = lax.broadcasted_iota(jnp.int32, (rows, HEAD), 0)
@@ -167,7 +216,8 @@
     def gather_owner(owner):
         peaks, totals, sums = [], [], []
         for j in range(seqs):
-            slots = [table_ref[(owner * seqs + j) * per_seq + k] for k in range(per_seq)]
+            spot = (owner * seqs + j) * per_seq
+            slots = [table_ref[spot // HEAD, spot % HEAD + k] for k in range(per_seq)]
             slot_peaks = [part_m[slot] for slot in slots]
             peak = functools.reduce(jnp.maximum, slot_peaks)
             factors = [jnp.exp(one - peak) for one in slot_peaks]
@@ -233,7 +283,7 @@
     for j in range(W_PARTS):
         loads[seqs + PAGE_PARTS + j].wait()
     width = weight_v.shape[1]
-    block = min(width, 256)
+    block = min(width, 512)
     share = all_seqs // tensors
 
     @pl.loop(0, width // block)
@@ -282,36 +332,35 @@
 def per_device(queries, cache, pages, page_owner, page_slot, lengths, out_weight):
     ranks = lax.axis_size("ranks")
     tensors = lax.axis_size("tensor")
-    me = lax.axis_index("ranks")
     seqs, width = queries.shape
     heads = width // HEAD
     page_count = pages.shape[0]
     kv_width = cache.shape[-1]
     resident = cache.shape[2]
     features = out_weight.shape[1]
-    own = me * page_count
-    place = lax.dynamic_slice_in_dim(
-        page_owner * page_count + page_slot, own, page_count, 0
-    )
-    seq_of_page = place // (page_count // seqs)
-    match = jnp.arange(ranks * page_count)[:, None] == place[None, :]
-    table = jnp.min(jnp.where(match, jnp.arange(page_count)[None, :], page_count), axis=1)
     all_seqs = ranks * seqs
     share = all_seqs // tensors
     folds = max(1, 16 // share)
     rows = seqs * heads
     slots = page_count + 1 + seqs
+    table_shape = (pl.cdiv(ranks * page_count, HEAD), HEAD)
     bf16, f32 = jnp.bfloat16, jnp.float32
-    smem = pl.BlockSpec(memory_space=pltpu.SMEM)
     vmem = pl.BlockSpec(memory_space=pltpu.VMEM)
-    hbm = pl.BlockSpec(memory_space=pl.ANY)
+    hbm = pl.BlockSpec(memory_space=pltpu.HBM)
     sems = pltpu.SemaphoreType.DMA
     return pl.pallas_call(
         functools.partial(kernel, ranks, tensors),
         out_shape=jax.ShapeDtypeStruct((share, features), bf16),
-        in_specs=[smem, smem, smem, vmem, hbm, hbm, hbm],
+        in_specs=[hbm, hbm, hbm, vmem, hbm, hbm, hbm],
         out_specs=vmem,
         scratch_shapes=[
+            pltpu.SMEM(page_owner.shape, jnp.int32),
+            pltpu.SMEM(page_slot.shape, jnp.int32),
+            pltpu.SMEM(lengths.shape, jnp.int32),
+            pltpu.VMEM(table_shape, jnp.int32),
+            pltpu.SMEM(table_shape, jnp.int32),
+            pltpu.VMEM((seqs, heads, HEAD), f32),
+            pltpu.VMEM((seqs, heads, HEAD), bf16),
             pltpu.VMEM(cache.shape, bf16),
             pltpu.VMEM(pages.shape, bf16),
             pltpu.VMEM(out_weight.shape, bf16),
@@ -331,6 +380,7 @@
             pltpu.VMEM((tensors, share, features), f32),
             pltpu.VMEM((tensors, share * folds, features // folds), bf16),
             pltpu.VMEM((tensors, share * folds, features // folds), bf16),
+            sems((4,)),
             sems((seqs + PAGE_PARTS + W_PARTS,)),
             sems((2, ranks)),
             sems((2, ranks)),
@@ -347,10 +397,10 @@
             transcendentals=0,
         ),
     )(
-        seq_of_page,
-        table,
+        page_owner,
+        page_slot,
         lengths,
-        queries.reshape(seqs, heads, HEAD),
+        queries,
         cache,
         pages,
         out_weight,

time: 35.7 us -> 29.4 us (0.82)
  Pallas kernels: 30.4 us -> 23.7 us
  local copies, waits for them, and re-layouts: 4.17 us -> 5.48 us
  other arithmetic: 0.85 us -> 0 us
    pallas_call x1, Pallas kernels: 30.4 us -> 23.7 us  [per_device(): pl.pallas_call(functools.partial(kernel, ranks, tensors), out_shape=jax.S...]
    unnamed x6 -> x11, local copies, waits for them, and re-layouts: 4.17 us -> 5.48 us
    add x1 -> x0, other arithmetic: 0.67 us -> none  [per_device(): page_owner * page_count + page_slot]
where the time goes in v2:
time: 29.4 us; the launch traced here: 29.1 us
  Pallas kernels  23.7 us (81%)
  local copies, waits for them, and re-layouts  5.48 us (19%)
    pallas_call x1, Pallas kernels, per_device(): pl.pallas_call(functools.partial(kernel, ranks, tensors), out_shape=jax.S...  23.7 us
    unnamed x11, local copies, waits for them, and re-layouts  5.48 us

profile of v2, /device:TPU:0, one launch (start us, length us, event | category | flops | bytes accessed | tf_op | source)
XLA Modules:
  0.0 29.1 jit_solution(17677814178664718503)
XLA Ops:
  0.0 0.0 copy-start
  0.0 2.2 %copy-done = bf16[4,2,1024,256]{3,2,1,0:T(8,128)(2,1)S(1)} copy-done((bf16[4,2,1024,256]{3,2,1,0:T(8,128)(2,1)S(1)}, bf16[4,2,1024,256]{3,2,1,0:T(8,128)(2,1)}, u32[]{:S(2)}) %copy-start) | copy-done | bytes 4194328
  2.2 0.0 copy-start.1
  2.2 0.7 %copy-done.1 = bf16[4,2048]{1,0:T(4,128)(2,1)S(1)} copy-done((bf16[4,2048]{1,0:T(4,128)(2,1)S(1)}, bf16[4,2048]{1,0:T(4,128)(2,1)}, u32[]{:S(2)}) %copy-start.1) | copy-done | bytes 16408
  2.9 0.0 copy-start.2
  2.9 0.7 %copy-done.2 = s32[128]{0:T(128)S(1)} copy-done((s32[128]{0:T(128)S(1)}, s32[128]{0:T(128)}, u32[]{:S(2)}) %copy-start.2) | copy-done | bytes 536
  3.6 0.0 copy-start.3
  3.6 0.7 %copy-done.3 = s32[128]{0:T(128)S(1)} copy-done((s32[128]{0:T(128)S(1)}, s32[128]{0:T(128)}, u32[]{:S(2)}) %copy-start.3) | copy-done | bytes 536
  4.2 0.0 copy-start.4
  4.2 0.7 %copy-done.4 = s32[4]{0:T(128)S(1)} copy-done((s32[4]{0:T(128)S(1)}, s32[4]{0:T(128)}, u32[]{:S(2)}) %copy-start.4) | copy-done | bytes 40
  4.9 23.7 %shard_map.73 = bf16[4,2048]{1,0:T(4,128)(2,1)S(1)} custom-call(s32[128]{0:T(128)S(1)} %copy-done.2, s32[128]{0:T(128)S(1)} %copy-done.3, s32[4]{0:T(128)S(1)} %copy-done.4, bf16[4,2048]{1,0:T(4,128)(2,1)S(1)} %copy-done.1, bf16[4,2,1024,256]{3,2,1,0:T(8,128)(2,1)S(1)} %copy-done, bf16[32,2,128,256]{3,2,1,0:T(8,128)(2,1)} %pages_hbm.1, ...), custom_call_target="tpu_custom_call" | custom-call | flops 134217728 | bytes 16777216 | tf_op jit(solution)/shard_map/pallas_call | solution.py:351
  28.5 0.6 %copy.9 = bf16[4,2048]{1,0:T(4,128)(2,1)} copy(bf16[4,2048]{1,0:T(4,128)(2,1)S(1)} %shard_map.73) | data formatting | bytes 32768
Async XLA Ops:
  0.0 2.2 %copy-start = (bf16[4,2,1024,256]{3,2,1,0:T(8,128)(2,1)S(1)}, bf16[4,2,1024,256]{3,2,1,0:T(8,128)(2,1)}, u32[]{:S(2)}) copy-start(bf16[4,2,1024,256]{3,2,1,0:T(8,128)(2,1)} %cache_hbm.1) | copy-start | bytes 12582916
  2.2 0.7 %copy-start.1 = (bf16[4,2048]{1,0:T(4,128)(2,1)S(1)}, bf16[4,2048]{1,0:T(4,128)(2,1)}, u32[]{:S(2)}) copy-start(bf16[4,2048]{1,0:T(4,128)(2,1)} %query_ref.1) | copy-start | bytes 49156
  2.9 0.7 %copy-start.2 = (s32[128]{0:T(128)S(1)}, s32[128]{0:T(128)}, u32[]{:S(2)}) copy-start(s32[128]{0:T(128)} %owner_hbm.1) | copy-start | bytes 1540
  3.6 0.7 %copy-start.3 = (s32[128]{0:T(128)S(1)}, s32[128]{0:T(128)}, u32[]{:S(2)}) copy-start(s32[128]{0:T(128)} %slot_hbm.1) | copy-start | bytes 1540
  4.2 0.7 %copy-start.4 = (s32[4]{0:T(128)S(1)}, s32[4]{0:T(128)}, u32[]{:S(2)}) copy-start(s32[4]{0:T(128)} %length_hbm.1) | copy-start | bytes 52

commit v3 on v2

--- a/solution.py
+++ b/solution.py
@@ -42,8 +42,6 @@
     part_l,
     o_send,
     o_recv,
-    ml_send,
-    ml_recv,
     att_send,
     att_recv,
     att_f32,
@@ -55,7 +53,6 @@
     load_sem,
     q_sems,
     o_sems,
-    ml_sems,
     att_sems,
     sum_sems,
 ):
@@ -226,15 +223,24 @@
             sums.append(sum(f * part_o[slot] for f, slot in zip(factors, slots)))
         return [jnp.concatenate(x, axis=0) for x in (peaks, totals, sums)]
 
-    o_copies, ml_copies = [], []
+    third = lax.broadcasted_iota(jnp.int32, (16, HEAD), 0)
+
+    def split(exact):
+        high = exact.astype(jnp.bfloat16).astype(jnp.float32)
+        rest = exact - high
+        middle = rest.astype(jnp.bfloat16).astype(jnp.float32)
+        low = rest - middle
+        tile = jnp.where(third == 2, low, 0.0)
+        tile = jnp.where(third == 1, middle, tile)
+        return jnp.where(third == 0, high, tile).astype(jnp.bfloat16)
+
+    o_copies = []
     for d in range(1, ranks):
         peak, total, mix = gather_owner(lax.rem(me + d, ranks))
-        o_send[d] = mix.astype(jnp.bfloat16)
+        o_send[d, :rows] = mix.astype(jnp.bfloat16)
         packed = jnp.where(low_diagonal, peak, jnp.where(high_diagonal, total, 0.0))
-        ml_send[d] = jnp.broadcast_to(jnp.sum(packed, axis=0, keepdims=True), (8, HEAD))
+        o_send[d, rows:] = split(jnp.sum(packed, axis=0, keepdims=True))
         o_copies.append(to_rank(d, o_send.at[d], o_recv, o_sems))
-        ml_copies.append(to_rank(d, ml_send.at[d], ml_recv, ml_sems))
-        ml_copies[-1].start()
         o_copies[-1].start()
 
     peak, total, mix = gather_owner(me)
@@ -251,9 +257,9 @@
 
     state = merge(*states)
     for d in range(1, ranks):
-        ml_copies[d - 1].wait_recv()
         o_copies[d - 1].wait_recv()
-        spread = jnp.broadcast_to(ml_recv[d, 0:1, :], (rows, HEAD))
+        exact = jnp.sum(o_recv[d, rows:].astype(jnp.float32), axis=0, keepdims=True)
+        spread = jnp.broadcast_to(exact, (rows, HEAD))
         peak = jnp.sum(jnp.where(low_diagonal, spread, 0.0), axis=1, keepdims=True)
         total = jnp.sum(jnp.where(high_diagonal, spread, 0.0), axis=1, keepdims=True)
         state = merge(
@@ -261,7 +267,7 @@
             (
                 jnp.broadcast_to(peak, (rows, HEAD)),
                 jnp.broadcast_to(total, (rows, HEAD)),
-                o_recv[d].astype(jnp.float32),
+                o_recv[d, :rows].astype(jnp.float32),
             ),
         )
     attended = (state[2] / state[1]).astype(jnp.bfloat16)
@@ -325,7 +331,7 @@
             c * share : (c + 1) * share
         ].astype(jnp.bfloat16)
 
-    for copy in q_copies + o_copies + ml_copies + att_copies + sum_copies:
+    for copy in q_copies + o_copies + att_copies + sum_copies:
         copy.wait_send()
 
 
@@ -369,10 +375,8 @@
             pltpu.VMEM((slots, heads, HEAD), f32),
             pltpu.VMEM((slots, heads, HEAD), f32),
             pltpu.VMEM((slots, heads, HEAD), f32),
-            pltpu.VMEM((ranks, rows, HEAD), bf16),
-            pltpu.VMEM((ranks, rows, HEAD), bf16),
-            pltpu.VMEM((ranks, 8, HEAD), f32),
-            pltpu.VMEM((ranks, 8, HEAD), f32),
+            pltpu.VMEM((ranks, rows + 16, HEAD), bf16),
+            pltpu.VMEM((ranks, rows + 16, HEAD), bf16),
             pltpu.VMEM((rows, HEAD), bf16),
             pltpu.VMEM((ranks, rows, HEAD), bf16),
             pltpu.VMEM((all_seqs, heads, HEAD), f32),
@@ -382,7 +386,6 @@
             pltpu.VMEM((tensors, share * folds, features // folds), bf16),
             sems((4,)),
             sems((seqs + PAGE_PARTS + W_PARTS,)),
-            sems((2, ranks)),
             sems((2, ranks)),
             sems((2, ranks)),
             sems((2, ranks)),

time: 29.4 us -> 29.3 us (level)
  no operation moved by 1% of the time
where the time goes in v3:
time: 29.3 us; the launch traced here: 29.1 us
  Pallas kernels  23.6 us (81%)
  local copies, waits for them, and re-layouts  5.48 us (19%)
    pallas_call x1, Pallas kernels, per_device(): pl.pallas_call(functools.partial(kernel, ranks, tensors), out_shape=jax.S...  23.6 us
    unnamed x11, local copies, waits for them, and re-layouts  5.48 us

profile of v3, /device:TPU:0, one launch (start us, length us, event | category | flops | bytes accessed | tf_op | source)
XLA Modules:
  0.0 29.1 jit_solution(12243661891326960083)
XLA Ops:
  0.0 0.0 copy-start
  0.0 2.2 %copy-done = bf16[4,2,1024,256]{3,2,1,0:T(8,128)(2,1)S(1)} copy-done((bf16[4,2,1024,256]{3,2,1,0:T(8,128)(2,1)S(1)}, bf16[4,2,1024,256]{3,2,1,0:T(8,128)(2,1)}, u32[]{:S(2)}) %copy-start) | copy-done | bytes 4194328
  2.2 0.0 copy-start.1
  2.2 0.7 %copy-done.1 = bf16[4,2048]{1,0:T(4,128)(2,1)S(1)} copy-done((bf16[4,2048]{1,0:T(4,128)(2,1)S(1)}, bf16[4,2048]{1,0:T(4,128)(2,1)}, u32[]{:S(2)}) %copy-start.1) | copy-done | bytes 16408
  2.9 0.0 copy-start.2
  2.9 0.7 %copy-done.2 = s32[128]{0:T(128)S(1)} copy-done((s32[128]{0:T(128)S(1)}, s32[128]{0:T(128)}, u32[]{:S(2)}) %copy-start.2) | copy-done | bytes 536
  3.6 0.0 copy-start.3
  3.6 0.7 %copy-done.3 = s32[128]{0:T(128)S(1)} copy-done((s32[128]{0:T(128)S(1)}, s32[128]{0:T(128)}, u32[]{:S(2)}) %copy-start.3) | copy-done | bytes 536
  4.2 0.0 copy-start.4
  4.2 0.7 %copy-done.4 = s32[4]{0:T(128)S(1)} copy-done((s32[4]{0:T(128)S(1)}, s32[4]{0:T(128)}, u32[]{:S(2)}) %copy-start.4) | copy-done | bytes 40
  4.9 23.6 %shard_map.73 = bf16[4,2048]{1,0:T(4,128)(2,1)S(1)} custom-call(s32[128]{0:T(128)S(1)} %copy-done.2, s32[128]{0:T(128)S(1)} %copy-done.3, s32[4]{0:T(128)S(1)} %copy-done.4, bf16[4,2048]{1,0:T(4,128)(2,1)S(1)} %copy-done.1, bf16[4,2,1024,256]{3,2,1,0:T(8,128)(2,1)S(1)} %copy-done, bf16[32,2,128,256]{3,2,1,0:T(8,128)(2,1)} %pages_hbm.1, ...), custom_call_target="tpu_custom_call" | custom-call | flops 134217728 | bytes 16777216 | tf_op jit(solution)/shard_map/pallas_call | solution.py:357
  28.5 0.6 %copy.9 = bf16[4,2048]{1,0:T(4,128)(2,1)} copy(bf16[4,2048]{1,0:T(4,128)(2,1)S(1)} %shard_map.73) | data formatting | bytes 32768
Async XLA Ops:
  0.0 2.2 %copy-start = (bf16[4,2,1024,256]{3,2,1,0:T(8,128)(2,1)S(1)}, bf16[4,2,1024,256]{3,2,1,0:T(8,128)(2,1)}, u32[]{:S(2)}) copy-start(bf16[4,2,1024,256]{3,2,1,0:T(8,128)(2,1)} %cache_hbm.1) | copy-start | bytes 12582916
  2.2 0.7 %copy-start.1 = (bf16[4,2048]{1,0:T(4,128)(2,1)S(1)}, bf16[4,2048]{1,0:T(4,128)(2,1)}, u32[]{:S(2)}) copy-start(bf16[4,2048]{1,0:T(4,128)(2,1)} %query_ref.1) | copy-start | bytes 49156
  2.9 0.7 %copy-start.2 = (s32[128]{0:T(128)S(1)}, s32[128]{0:T(128)}, u32[]{:S(2)}) copy-start(s32[128]{0:T(128)} %owner_hbm.1) | copy-start | bytes 1540
  3.6 0.7 %copy-start.3 = (s32[128]{0:T(128)S(1)}, s32[128]{0:T(128)}, u32[]{:S(2)}) copy-start(s32[128]{0:T(128)} %slot_hbm.1) | copy-start | bytes 1540
  4.2 0.7 %copy-start.4 = (s32[4]{0:T(128)S(1)}, s32[4]{0:T(128)}, u32[]{:S(2)}) copy-start(s32[4]{0:T(128)} %length_hbm.1) | copy-start | bytes 52

commit v4 on v3

--- a/solution.py
+++ b/solution.py
@@ -11,7 +11,7 @@
 MESH = pl.DeviceIdType.MESH
 LOWEST = -1e30
 W_PARTS = 4
-PAGE_PARTS = 4
+PAGE_PARTS = 1
 
 
 def kernel(
@@ -289,7 +289,7 @@
     for j in range(W_PARTS):
         loads[seqs + PAGE_PARTS + j].wait()
     width = weight_v.shape[1]
-    block = min(width, 512)
+    block = min(width, 1024)
     share = all_seqs // tensors
 
     @pl.loop(0, width // block)

time: 29.3 us -> 28.2 us (0.962)
  Pallas kernels: 23.6 us -> 22.4 us
    pallas_call x1, Pallas kernels: 23.6 us -> 22.4 us  [per_device(): pl.pallas_call(functools.partial(kernel, ranks, tensors), out_shape=jax.S...]
where the time goes in v4:
time: 28.2 us; the launch traced here: 27.9 us
  Pallas kernels  22.4 us (79%)
  local copies, waits for them, and re-layouts  5.48 us (19%)
    pallas_call x1, Pallas kernels, per_device(): pl.pallas_call(functools.partial(kernel, ranks, tensors), out_shape=jax.S...  22.4 us
    unnamed x11, local copies, waits for them, and re-layouts  5.48 us

profile of v4, /device:TPU:0, one launch (start us, length us, event | category | flops | bytes accessed | tf_op | source)
XLA Modules:
  0.0 27.9 jit_solution(16223958330188397486)
XLA Ops:
  0.0 0.0 copy-start
  0.0 2.2 %copy-done = bf16[4,2,1024,256]{3,2,1,0:T(8,128)(2,1)S(1)} copy-done((bf16[4,2,1024,256]{3,2,1,0:T(8,128)(2,1)S(1)}, bf16[4,2,1024,256]{3,2,1,0:T(8,128)(2,1)}, u32[]{:S(2)}) %copy-start) | copy-done | bytes 4194328
  2.2 0.0 copy-start.1
  2.2 0.7 %copy-done.1 = bf16[4,2048]{1,0:T(4,128)(2,1)S(1)} copy-done((bf16[4,2048]{1,0:T(4,128)(2,1)S(1)}, bf16[4,2048]{1,0:T(4,128)(2,1)}, u32[]{:S(2)}) %copy-start.1) | copy-done | bytes 16408
  2.9 0.0 copy-start.2
  2.9 0.7 %copy-done.2 = s32[128]{0:T(128)S(1)} copy-done((s32[128]{0:T(128)S(1)}, s32[128]{0:T(128)}, u32[]{:S(2)}) %copy-start.2) | copy-done | bytes 536
  3.6 0.0 copy-start.3
  3.6 0.7 %copy-done.3 = s32[128]{0:T(128)S(1)} copy-done((s32[128]{0:T(128)S(1)}, s32[128]{0:T(128)}, u32[]{:S(2)}) %copy-start.3) | copy-done | bytes 536
  4.2 0.0 copy-start.4
  4.2 0.7 %copy-done.4 = s32[4]{0:T(128)S(1)} copy-done((s32[4]{0:T(128)S(1)}, s32[4]{0:T(128)}, u32[]{:S(2)}) %copy-start.4) | copy-done | bytes 40
  4.9 22.4 %shard_map.73 = bf16[4,2048]{1,0:T(4,128)(2,1)S(1)} custom-call(s32[128]{0:T(128)S(1)} %copy-done.2, s32[128]{0:T(128)S(1)} %copy-done.3, s32[4]{0:T(128)S(1)} %copy-done.4, bf16[4,2048]{1,0:T(4,128)(2,1)S(1)} %copy-done.1, bf16[4,2,1024,256]{3,2,1,0:T(8,128)(2,1)S(1)} %copy-done, bf16[32,2,128,256]{3,2,1,0:T(8,128)(2,1)} %pages_hbm.1, ...), custom_call_target="tpu_custom_call" | custom-call | flops 134217728 | bytes 16777216 | tf_op jit(solution)/shard_map/pallas_call | solution.py:357
  27.3 0.6 %copy.9 = bf16[4,2048]{1,0:T(4,128)(2,1)} copy(bf16[4,2048]{1,0:T(4,128)(2,1)S(1)} %shard_map.73) | data formatting | bytes 32768
Async XLA Ops:
  0.0 2.2 %copy-start = (bf16[4,2,1024,256]{3,2,1,0:T(8,128)(2,1)S(1)}, bf16[4,2,1024,256]{3,2,1,0:T(8,128)(2,1)}, u32[]{:S(2)}) copy-start(bf16[4,2,1024,256]{3,2,1,0:T(8,128)(2,1)} %cache_hbm.1) | copy-start | bytes 12582916
  2.2 0.7 %copy-start.1 = (bf16[4,2048]{1,0:T(4,128)(2,1)S(1)}, bf16[4,2048]{1,0:T(4,128)(2,1)}, u32[]{:S(2)}) copy-start(bf16[4,2048]{1,0:T(4,128)(2,1)} %query_ref.1) | copy-start | bytes 49156
  2.9 0.7 %copy-start.2 = (s32[128]{0:T(128)S(1)}, s32[128]{0:T(128)}, u32[]{:S(2)}) copy-start(s32[128]{0:T(128)} %owner_hbm.1) | copy-start | bytes 1540
  3.6 0.7 %copy-start.3 = (s32[128]{0:T(128)S(1)}, s32[128]{0:T(128)}, u32[]{:S(2)}) copy-start(s32[128]{0:T(128)} %slot_hbm.1) | copy-start | bytes 1540
  4.2 0.7 %copy-start.4 = (s32[4]{0:T(128)S(1)}, s32[4]{0:T(128)}, u32[]{:S(2)}) copy-start(s32[4]{0:T(128)} %length_hbm.1) | copy-start | bytes 52
